TPU v7x, 32 devices: a whole 2x2x4 slice. The times are simulated.
32 devices in a mesh: chan: 16 (over z, y, x), freq: 2 (over core).
Axes of the slice: x: 2, y: 2, z: 4, core: 2. Of those that a mesh axis runs over, the one named last changes fastest.
Arguments:
- spectra: bfloat16 [256, 2, 16, 2048], P('freq', None, None, 'chan'), may hold values from -20 to 20
- model: bfloat16 [256, 2, 8, 2048], P('freq', None, None, 'chan'), may hold values from -6 to 6
- channel_ok: int32 [2048], replicated, may hold values 0 or 1
- limits: int32 [16], replicated, may hold values from 128 to 1024, as said below
Outputs:
- adjoint: float32 [256, 2, 16, 2048], P('freq', None, None, 'chan')
- misfit: float32 [], replicated
Inputs may be any that keep to these rules, and one draw needn't show every extreme that they name: `limits`: one block has the limit 128 and another the limit 1024.
All inputs are finite; a program needn't handle non-finite values.
Results may differ from a plain program's by a relative error of at most 0.00053.
Values may be sent and summed in bfloat16 or wider, within the bound.
No kernel may reach another device: no remote copies, remote signals or barrier semaphores. Data moves between devices by JAX's collectives and lax.ppermute only.
A program may use at most 192 MiB of HBM per device.

v0:
```python
import functools
import math

import jax
import jax.numpy as jnp
from jax import lax
from jax.experimental import pallas as pl
from jax.experimental.pallas import tpu as pltpu
from jax.sharding import PartitionSpec as P

W = 16
BAND = 1024
CHUNKS = 2
UNROLL = 32
REST = 16
SELF_UNROLL = 16
EXTRA_ROWS = 8
MISFIT_ROWS = 4


def power_below(top):
    return jnp.ceil(jnp.log(jnp.maximum(top, 1e-30)) * (1.0 / math.log(2.0)))


def scaled_rows(adjoint, misfit):
    bins, rows, width = adjoint.shape
    exponent = power_below(jnp.max(jnp.abs(adjoint), axis=1, keepdims=True))
    scaled = adjoint * jnp.exp2(15.0 - exponent)
    misfit = jnp.sum(misfit, axis=0, keepdims=True)
    misfit = misfit[:, :width] + misfit[:, width:]
    power = power_below(misfit)
    rest = misfit * jnp.exp2(10.0 - power)
    lines = [exponent[f] for f in range(bins)]
    lines += [jnp.zeros_like(misfit)] * (EXTRA_ROWS - MISFIT_ROWS - bins) + [power]
    for _ in range(2):
        lines.append(jnp.floor(rest))
        rest = (rest - jnp.floor(rest)) * 1024.0
    lines.append(rest)
    place = lax.broadcasted_iota(jnp.int32, (EXTRA_ROWS, width), 0)
    extra = jnp.zeros((EXTRA_ROWS, width), jnp.float32)
    for n, line in enumerate(lines):
        extra = jnp.where(place == n, line, extra)
    return jnp.concatenate([scaled.reshape(bins * rows, width), extra], axis=0)


def unscaled(packed, bins):
    blocks, _, width = packed.shape
    values = packed[:, : bins * 2 * W].astype(jnp.float32).reshape(blocks, bins, 2 * W, width)
    exponents = packed[:, bins * 2 * W : bins * 2 * W + bins].astype(jnp.float32)
    return values * jnp.exp2(exponents - 15.0)[:, :, None]


def unscaled_misfit(packed):
    power, high, middle, low = [packed[:, n - MISFIT_ROWS].astype(jnp.float32) for n in range(MISFIT_ROWS)]
    return jnp.sum((high + middle * 2.0**-10 + low * 2.0**-20) * jnp.exp2(power - 10.0))


def expanded(x):
    terms = (x.shape[0] - 2 * W) // 2
    sr, si, mr, mi = x[:W], x[W : 2 * W], x[2 * W : 2 * W + terms], x[2 * W + terms :]
    turned = jnp.concatenate([-si, sr, -mi, mr], axis=0)
    scaled = jnp.concatenate([x[: 2 * W] * (1.0 / W), -x[2 * W :]], axis=0)
    return x.astype(jnp.bfloat16), turned.astype(jnp.bfloat16), scaled.T.astype(jnp.bfloat16)


def squares(r):
    return jnp.sum((r * r).reshape(r.shape[0] // 8, 8, r.shape[1]), axis=0)


def apply_rows(w, r):
    return lax.dot_general(w[: 2 * W], r, (((1,), (1,)), ((), ())), preferred_element_type=jnp.float32)


def self_kernel(ok_ref, spectra_ref, model_ref, out_ref, mis_ref, *, unroll):
    bin_total, _, width = spectra_ref.shape
    row = lax.broadcasted_iota(jnp.int32, (width, 2 * width), 0)
    col = lax.broadcasted_iota(jnp.int32, (width, 2 * width), 1) % width
    ok = ok_ref[...].astype(jnp.float32)
    mis_ref[...] = jnp.zeros_like(mis_ref)

    def step(t, carry):
        total = jnp.zeros(mis_ref.shape, jnp.float32)
        for i in range(unroll):
            f = t * unroll + i
            x = jnp.concatenate([spectra_ref[f].astype(jnp.float32), model_ref[f].astype(jnp.float32)], axis=0) * ok
            x, turned, left = expanded(x)
            w = jnp.concatenate([x, turned], axis=1)
            r = jnp.dot(left, w, preferred_element_type=jnp.float32)
            r = jnp.where(row != col, r, 0.0)
            total += squares(r)
            out_ref[f] = apply_rows(w, r.astype(jnp.bfloat16)) * (1.0 / W)
        mis_ref[...] += total * 0.5
        return carry

    lax.fori_loop(0, bin_total // unroll, step, 0)


def self_call(ok, spectra, model):
    bin_total, _, width = spectra.shape
    vmem = pl.BlockSpec(memory_space=pltpu.VMEM)
    return pl.pallas_call(
        functools.partial(self_kernel, unroll=math.gcd(bin_total, SELF_UNROLL)),
        out_shape=(
            jax.ShapeDtypeStruct((bin_total, 2 * W, width), jnp.float32),
            jax.ShapeDtypeStruct((8, 2 * width), jnp.float32),
        ),
        in_specs=[vmem, vmem, vmem],
        out_specs=(vmem, vmem),
        compiler_params=pltpu.CompilerParams(vmem_limit_bytes=40 * 2**20),
        name="own_block",
    )(ok, spectra, model)


def band_kernel(limits_ref, ok_ref, before_ref, x_ref, out_ref, mis_ref, wt_ref, at_ref, acc_ref, own_ref, far_ref, r0_ref, r1_ref, t0_ref, t1_ref, *, firsts, wrap, pack):
    blocks, bins, rows, width = x_ref.shape
    unroll = max(2, UNROLL // bins // 2 * 2)
    rest = max(2, REST // bins // 2 * 2)
    slots = (r0_ref, r1_ref)
    turned_slots = (t0_ref, t1_ref)
    acc_ref[...] = jnp.zeros_like(acc_ref)

    def prepare(b, carry):
        ok = ok_ref[b].astype(jnp.float32)
        for f in range(bins):
            x, turned, left = expanded(x_ref[b, f].astype(jnp.float32) * ok)
            wt_ref[b, f, :, :width] = x
            wt_ref[b, f, :, width:] = turned
            at_ref[b, f] = left
        own_ref[b] = jnp.zeros_like(own_ref[b])
        far_ref[b] = jnp.zeros_like(far_ref[b])
        return carry

    lax.fori_loop(0, blocks, prepare, 0, unroll=math.gcd(blocks, 4))

    row = lax.broadcasted_iota(jnp.int32, (width, 2 * width), 0)
    col = lax.broadcasted_iota(jnp.int32, (width, 2 * width), 1) % width
    diff = col - row

    def last_piece(b):
        return (limits_ref[b] + width - 1) // width

    def next_item(b, s):
        done = (b >= firsts) | (s >= last_piece(jnp.minimum(b, firsts - 1)))
        return jnp.where(done, b + 1, b), jnp.where(done, 1, s + 1)

    def blocks_of(b, s):
        b = jnp.minimum(b, firsts - 1)
        j = b + s
        if wrap:
            j = jnp.where(j >= blocks, j - blocks, j)
        return b, j

    def cross(slot, item):
        b, s = item
        live = b < firsts
        b, j = blocks_of(b, s)
        mask = diff <= jnp.where(live, limits_ref[b] - s * width, -width)
        for f in range(bins):
            r = jnp.dot(at_ref[b, f], wt_ref[j, f], preferred_element_type=jnp.float32)
            r = jnp.where(mask, r, 0.0)
            acc_ref[f] += squares(r)
            r = r.astype(jnp.bfloat16)
            slots[slot][f] = r
            if f % 2:
                turned_slots[slot][f, :, :width] = r[:, :width].T
                turned_slots[slot][f, :, width:] = r[:, width:].T

    def adjoint(slot, item):
        b, j = blocks_of(*item)
        for f in range(bins):
            r = slots[slot][f]
            if f % 2:
                own = jnp.dot(wt_ref[j, f, : 2 * W, :width], turned_slots[slot][f], preferred_element_type=jnp.float32)
                own_ref[b, f, :W] += own[:W, :width] - own[W:, width:]
                own_ref[b, f, W:] += own[W:, :width] + own[:W, width:]
            else:
                own_ref[b, f] += apply_rows(wt_ref[j, f], r)
            far = jnp.dot(wt_ref[b, f, : 2 * W, :width], r, preferred_element_type=jnp.float32)
            far_ref[j, f, :W] += far[:W, :width] + far[W:, width:]
            far_ref[j, f, W:] += far[W:, :width] - far[:W, width:]

    def step(count, _, item):
        for i in range(count):
            later = next_item(*item)
            cross((i + 1) % 2, later)
            adjoint(i % 2, item)
            item = later
        return item

    total = lax.fori_loop(0, firsts, lambda b, n: n + last_piece(b), jnp.int32(0))
    first = (jnp.int32(0), jnp.int32(1))
    cross(0, first)
    if rest == unroll:
        lax.fori_loop(0, (total + unroll - 1) // unroll, functools.partial(step, unroll), first)
    else:
        item = lax.fori_loop(0, total // unroll, functools.partial(step, unroll), first)
        lax.fori_loop(0, (total % unroll + rest - 1) // rest, functools.partial(step, rest), item)

    mis_ref[...] = before_ref[...] + jnp.sum(acc_ref[...], axis=0)

    def finish(b, carry):
        result = (own_ref[b] + far_ref[b]) * (1.0 / W)
        out_ref[b] = scaled_rows(result, mis_ref[...]) if pack else result
        return carry

    lax.fori_loop(0, blocks, finish, 0, unroll=math.gcd(blocks, 2))


def band_call(limits, ok, before, x, firsts, wrap, pack):
    blocks, bins, rows, width = x.shape
    out_shape = (blocks, bins * 2 * W + EXTRA_ROWS, width) if pack else (blocks, bins, 2 * W, width)
    vmem = pl.BlockSpec(memory_space=pltpu.VMEM)
    smem = pl.BlockSpec(memory_space=pltpu.SMEM)
    return pl.pallas_call(
        functools.partial(band_kernel, firsts=firsts, wrap=wrap, pack=pack),
        out_shape=(
            jax.ShapeDtypeStruct(out_shape, jnp.float32),
            jax.ShapeDtypeStruct(before.shape, jnp.float32),
        ),
        in_specs=[smem, vmem, vmem, vmem],
        out_specs=(vmem, vmem),
        scratch_shapes=[
            pltpu.VMEM((blocks, bins, rows, 2 * width), jnp.bfloat16),
            pltpu.VMEM((blocks, bins, width, rows), jnp.bfloat16),
            pltpu.VMEM((bins, 8, 2 * width), jnp.float32),
            pltpu.VMEM((blocks, bins, 2 * W, width), jnp.float32),
            pltpu.VMEM((blocks, bins, 2 * W, width), jnp.float32),
            pltpu.VMEM((bins, width, 2 * width), jnp.bfloat16),
            pltpu.VMEM((bins, width, 2 * width), jnp.bfloat16),
            pltpu.VMEM((bins, width, 2 * width), jnp.bfloat16),
            pltpu.VMEM((bins, width, 2 * width), jnp.bfloat16),
        ],
        compiler_params=pltpu.CompilerParams(vmem_limit_bytes=40 * 2**20),
        name="band",
    )(limits, ok, before, x)


def sum_over(x, axis, reach=1):
    peers = lax.axis_size(axis)
    if reach == peers:
        return x
    if (peers // reach) & (peers // reach - 1):
        return lax.psum(x, axis) / reach
    while reach < peers:
        x = x + lax.ppermute(x, axis, [(i, i // (2 * reach) * 2 * reach + (i + reach) % (2 * reach)) for i in range(peers)])
        reach *= 2
    return x


def shards(spectra, model, channel_ok, limits):
    bin_total, _, _, width = spectra.shape
    peers = lax.axis_size("chan")
    here = lax.axis_index("chan")
    band_blocks = BAND // width
    group = max(g for g in range(1, peers + 1) if peers % g == 0 and bin_total % g == 0)
    wrap = group == peers
    groups = None if wrap else [[start + i for i in range(group)] for start in range(0, peers, group)]
    per_device = bin_total // group
    chunks = math.gcd(CHUNKS, per_device)
    bins = per_device // chunks
    chunk_bins = bin_total // chunks

    ok = channel_ok.reshape(peers, 1, width)
    ok_here = lax.dynamic_index_in_dim(ok, here, keepdims=False)
    if not wrap:
        start = here // group * group
        limits = lax.dynamic_slice_in_dim(limits, start, group)
        ok = lax.dynamic_slice_in_dim(jnp.concatenate([ok, ok]), start, group + band_blocks)
    arrays = spectra.reshape(bin_total, -1, width), model.reshape(bin_total, -1, width)
    rows = arrays[0].shape[1] + arrays[1].shape[1]

    def swap(x):
        return lax.all_to_all(x, "chan", 0, 0, axis_index_groups=groups, tiled=True)

    def halo_move(x, by):
        return lax.ppermute(x, "chan", [(i, (i + by) % peers) for i in range(peers)])

    adjoint, misfit = self_call(ok_here, *arrays)
    inbound = []
    after = misfit
    for c in range(chunks):
        if c:
            arrays, after = lax.optimization_barrier((arrays, after))
        inbound.append(swap(jnp.concatenate([x[c * chunk_bins : (c + 1) * chunk_bins] for x in arrays], axis=1)))
    outbound = []
    for c in range(chunks):
        part = inbound[c]
        if c:
            part, outbound[-1] = lax.optimization_barrier((part, outbound[-1]))
        part = part.reshape(group, bins, rows, width)
        if not wrap:
            part = jnp.concatenate([part, halo_move(part[:band_blocks], -group)], axis=0)
        packed, misfit = band_call(limits, ok, misfit, part, group, wrap, wrap)
        if not wrap:
            back = halo_move(packed[group:], group)
            packed = jnp.concatenate([packed[:band_blocks] + back, packed[band_blocks:group]], axis=0)
            packed = jax.vmap(scaled_rows, (0, None))(packed, misfit)
        outbound.append(packed.astype(jnp.float16))
    for c in range(chunks):
        packed = outbound[c]
        if c:
            packed, arrived = lax.optimization_barrier((packed, arrived))
        packed = swap(packed)
        arrived = packed
        part = unscaled(packed, bins).reshape(chunk_bins, 2 * W, width)
        part = part + lax.slice_in_dim(adjoint, c * chunk_bins, (c + 1) * chunk_bins)
        adjoint = lax.dynamic_update_slice_in_dim(adjoint, part, c * chunk_bins, 0)
    misfit = sum_over(sum_over(unscaled_misfit(packed), "freq"), "chan", group)
    misfit = misfit / float(2 * bin_total * lax.axis_size("freq") * peers * width * BAND)
    return adjoint.reshape(spectra.shape), misfit


def solution(mesh):
    return jax.shard_map(
        shards,
        mesh=mesh,
        in_specs=(P("freq", None, None, "chan"), P("freq", None, None, "chan"), P(), P()),
        out_specs=(P("freq", None, None, "chan"), P()),
        check_vma=False,
    )
```

profile of v0, /device:TPU:0, one launch (start us, length us, event | category | flops | bytes accessed | tf_op | source)
XLA Modules:
  0.0 104.0 jit_solution(550085371588856785)
XLA Ops:
  0.6 0.0 slice-start
  0.6 1.0 slice_bitcast_fusion
  1.7 0.1 slice-done
  1.8 0.0 copy-start.2
  1.8 0.0 copy-start
  1.8 0.0 copy-start.1
  1.8 1.0 pad_maximum_fusion.1
  2.7 8.3 %all-to-all-start.1 = ((bf16[64,48,128]{2,1,0:T(8,128)(2,1)}), bf16[64,48,128]{2,1,0:T(8,128)(2,1)S(1)}, u32[]{:S(2)}, u32[]{:S(2)}) async-start(bf16[64,48,128]{2,1,0:T(8,128)(2,1)} %pad_maximum_fusion.1), calls=%async_computation.1 | async-start | bytes 1572864 | tf_op jit(solution)/shard_map/all_to_all | solution.py:273
  11.1 0.0 copy-done.2
  11.1 0.0 copy-done
  11.1 0.0 copy-done.1
  11.1 8.3 %own_block.1 = (f32[128,32,128]{2,1,0:T(8,128)}, f32[8,256]{1,0:T(8,128)S(1)}) custom-call(s32[1,128]{1,0:T(1,128)S(1)} %fusion.12.ok_ref, bf16[128,32,128]{2,1,0:T(8,128)(2,1)S(1)} %bitcast.17, bf16[128,16,128]{2,1,0:T(8,128)(2,1)S(1)} %bitcast.22), custom_call_target="tpu_custom_call" | custom-call | tf_op jit(solution)/shard_map/own_block/pallas_call | solution.py:101
  19.5 0.0 copy-start.3
  19.5 0.9 pad_maximum_fusion
  20.4 10.4 %all-to-all-done.1 = bf16[64,48,128]{2,1,0:T(8,128)(2,1)S(1)} async-done(((bf16[64,48,128]{2,1,0:T(8,128)(2,1)}), bf16[64,48,128]{2,1,0:T(8,128)(2,1)S(1)}, u32[]{:S(2)}, u32[]{:S(2)}) %all-to-all-start.1) | async-done | bytes 786464 | tf_op jit(solution)/shard_map/all_to_all | solution.py:273
  30.8 4.9 %all-to-all-start = ((bf16[64,48,128]{2,1,0:T(8,128)(2,1)}), bf16[64,48,128]{2,1,0:T(8,128)(2,1)S(1)}, u32[]{:S(2)}, u32[]{:S(2)}) async-start(bf16[64,48,128]{2,1,0:T(8,128)(2,1)} %pad_maximum_fusion), calls=%async_computation | async-start | bytes 1572864 | tf_op jit(solution)/shard_map/all_to_all | solution.py:273
  35.7 0.0 copy-done.3
  35.7 17.1 %band.2 = (f32[16,136,128]{2,1,0:T(8,128)S(1)}, f32[8,256]{1,0:T(8,128)S(1)}) custom-call(s32[16]{0:T(128)S(1)} %copy-done.3, s32[16,1,128]{2,1,0:T(1,128)S(1)} %bitcast.25, f32[8,256]{1,0:T(8,128)S(1)} %get-tuple-element.13.before_ref, bf16[16,4,48,128]{3,2,1,0:T(8,128)(2,1)S(1)} %bitcast.20), custom_call_target="tpu_custom_call" | custom-call | tf_op jit(solution)/shard_map/band/pallas_call | solution.py:214
  52.8 0.9 convert_element_type.30
  53.7 0.6 all-to-all-done
  54.3 6.2 %all-to-all-start.2 = ((f16[16,136,128]{2,1,0:T(8,128)(2,1)}), f16[16,136,128]{2,1,0:T(8,128)(2,1)S(1)}, u32[]{:S(2)}, u32[]{:S(2)}) async-start(f16[16,136,128]{2,1,0:T(8,128)(2,1)} %convert_element_type.30), calls=%async_computation.2 | async-start | bytes 1114112 | tf_op jit(solution)/shard_map/all_to_all | solution.py:273
  60.5 17.6 %band.3 = (f32[16,136,128]{2,1,0:T(8,128)S(1)}, f32[8,256]{1,0:T(8,128)}) custom-call(s32[16]{0:T(128)S(1)} %copy-done.3, s32[16,1,128]{2,1,0:T(1,128)S(1)} %bitcast.26, f32[8,256]{1,0:T(8,128)S(1)} %get-tuple-element.18.before_ref, bf16[16,4,48,128]{3,2,1,0:T(8,128)(2,1)S(1)} %bitcast.21), custom_call_target="tpu_custom_call" | custom-call | tf_op jit(solution)/shard_map/band/pallas_call | solution.py:214
  78.2 0.0 copy-start.4
  78.2 0.9 convert_element_type.32
  79.1 0.0 all-to-all-done.2
  79.1 6.9 %all-to-all-start.3 = ((f16[16,136,128]{2,1,0:T(8,128)(2,1)}), f16[16,136,128]{2,1,0:T(8,128)(2,1)S(1)}, u32[]{:S(2)}, u32[]{:S(2)}) async-start(f16[16,136,128]{2,1,0:T(8,128)(2,1)} %convert_element_type.32), calls=%async_computation.3 | async-start | bytes 1114112 | tf_op jit(solution)/shard_map/all_to_all | solution.py:273
  86.0 0.1 slice.64
  86.2 0.0 copy-done.4
  86.2 0.4 fusion.2
  86.6 13.1 %all-to-all-done.3 = f16[16,136,128]{2,1,0:T(8,128)(2,1)S(1)} async-done(((f16[16,136,128]{2,1,0:T(8,128)(2,1)}), f16[16,136,128]{2,1,0:T(8,128)(2,1)S(1)}, u32[]{:S(2)}, u32[]{:S(2)}) %all-to-all-start.3) | async-done | bytes 557088 | tf_op jit(solution)/shard_map/all_to_all | solution.py:273
  99.6 0.6 fusion.11
  100.3 0.0 collective-permute-start
  100.3 0.1 slice.66
  100.4 0.4 fusion
  100.8 0.0 copy-start.5
  100.8 0.8 collective-permute-done
  102.9 0.0 copy-done.5
  (5 shorter events, 0.1 us)
Async XLA Ops:
  0.6 1.1 %slice-start = ((bf16[128,2,16,128]{3,2,1,0:T(8,128)(2,1)}), bf16[64,2,16,128]{3,2,1,0:T(8,128)(2,1)S(1)}, s32[]{:S(2)}) async-start(bf16[128,2,16,128]{3,2,1,0:T(8,128)(2,1)} %param.4), calls=%async_computation.4 | async-start | bytes 1048576 | tf_op jit(solution)/shard_map/slice | solution.py:284
  1.8 9.3 %copy-start.2 = (s32[2048]{0:T(1024)S(1)}, s32[2048]{0:T(1024)}, u32[]{:S(2)}) copy-start(s32[2048]{0:T(1024)} %param.6) | copy-start | bytes 24580
  1.8 9.3 %copy-start = (bf16[128,2,16,128]{3,2,1,0:T(8,128)(2,1)S(1)}, bf16[128,2,16,128]{3,2,1,0:T(8,128)(2,1)}, u32[]{:S(2)}) copy-start(bf16[128,2,16,128]{3,2,1,0:T(8,128)(2,1)} %param.4) | copy-start | bytes 3145732
  1.8 9.3 %copy-start.1 = (bf16[128,2,8,128]{3,2,1,0:T(8,128)(2,1)S(1)}, bf16[128,2,8,128]{3,2,1,0:T(8,128)(2,1)}, u32[]{:S(2)}) copy-start(bf16[128,2,8,128]{3,2,1,0:T(8,128)(2,1)} %param.5) | copy-start | bytes 1572868
  2.7 28.1 %all-to-all-start.1 = ((bf16[64,48,128]{2,1,0:T(8,128)(2,1)}), bf16[64,48,128]{2,1,0:T(8,128)(2,1)S(1)}, u32[]{:S(2)}, u32[]{:S(2)}) async-start(bf16[64,48,128]{2,1,0:T(8,128)(2,1)} %pad_maximum_fusion.1), calls=%async_computation.1 | async-start | bytes 1572864 | tf_op jit(solution)/shard_map/all_to_all | solution.py:273
  19.5 16.2 %copy-start.3 = (s32[16]{0:T(128)S(1)}, s32[16]{0:T(128)}, u32[]{:S(2)}) copy-start(s32[16]{0:T(128)} %limits_ref.3) | copy-start | bytes 196
  30.8 23.5 %all-to-all-start = ((bf16[64,48,128]{2,1,0:T(8,128)(2,1)}), bf16[64,48,128]{2,1,0:T(8,128)(2,1)S(1)}, u32[]{:S(2)}, u32[]{:S(2)}) async-start(bf16[64,48,128]{2,1,0:T(8,128)(2,1)} %pad_maximum_fusion), calls=%async_computation | async-start | bytes 1572864 | tf_op jit(solution)/shard_map/all_to_all | solution.py:273
  54.3 24.7 %all-to-all-start.2 = ((f16[16,136,128]{2,1,0:T(8,128)(2,1)}), f16[16,136,128]{2,1,0:T(8,128)(2,1)S(1)}, u32[]{:S(2)}, u32[]{:S(2)}) async-start(f16[16,136,128]{2,1,0:T(8,128)(2,1)} %convert_element_type.30), calls=%async_computation.2 | async-start | bytes 1114112 | tf_op jit(solution)/shard_map/all_to_all | solution.py:273
  78.2 8.0 %copy-start.4 = (f32[128,32,128]{2,1,0:T(8,128)S(1)}, f32[128,32,128]{2,1,0:T(8,128)}, u32[]{:S(2)}) copy-start(f32[128,32,128]{2,1,0:T(8,128)} %get-tuple-element.12) | copy-start | bytes 6291460
  79.1 20.5 %all-to-all-start.3 = ((f16[16,136,128]{2,1,0:T(8,128)(2,1)}), f16[16,136,128]{2,1,0:T(8,128)(2,1)S(1)}, u32[]{:S(2)}, u32[]{:S(2)}) async-start(f16[16,136,128]{2,1,0:T(8,128)(2,1)} %convert_element_type.32), calls=%async_computation.3 | async-start | bytes 1114112 | tf_op jit(solution)/shard_map/all_to_all | solution.py:273
  100.3 1.4 %collective-permute-start = (f32[]{:T(128)}, f32[]{:T(128)}, u32[]{:S(2)}, u32[]{:S(2)}) collective-permute-start(f32[]{:T(128)} %fusion.11), channel_id=1, source_target_pairs={{0,1},{1,0},{2,3},{3,2},{4,5},{5,4},{6,7},{7,6},{8,9},{9,8},{10,11... | collective-permute-start | bytes 20 | tf_op jit(solution)/shard_map/ppermute | solution.py:245
  100.8 2.0 %copy-start.5 = (f32[128,32,128]{2,1,0:T(8,128)}, f32[128,32,128]{2,1,0:T(8,128)S(1)}, u32[]{:S(2)}) copy-start(f32[128,32,128]{2,1,0:T(8,128)S(1)} %fusion) | copy-start | bytes 6291460
where the time goes:
time: 103 us; the launch traced here: 104 us
  Pallas kernels  43 us (42%)
  starting transfers between devices  26.3 us (26%)
  waiting for transfers between devices  24.9 us (24%)
  other arithmetic  5.16 us (5%)
  between operations  3.13 us (3%)
  local copies, waits for them, and re-layouts  1.45 us (1%)
    pallas_call x2, Pallas kernels, band_call(): pl.pallas_call(functools.partial(band_kernel, firsts=firsts, wrap=wrap, p...  34.7 us
    all_to_all x4, starting transfers between devices, swap(): return lax.all_to_all(x, 'chan', 0, 0, axis_index_groups=groups, tiled=True)  26.3 us
    all_to_all x4, waiting for transfers between devices, swap(): return lax.all_to_all(x, 'chan', 0, 0, axis_index_groups=groups, tiled=True)  24.1 us
    pallas_call x1, Pallas kernels, self_call(): pl.pallas_call(functools.partial(self_kernel, unroll=math.gcd(bin_total,...  8.3 us
  transfers between devices with their start and end apart: 5, of which 4 were waited for; matrix products, arithmetic and copies ran while one was open for 4% of the time, Pallas kernels for 41%

commit v1 on v0

--- a/solution.py
+++ b/solution.py
@@ -11,7 +11,9 @@
 W = 16
 BAND = 1024
 CHUNKS = 2
-UNROLL = 32
+UNROLL = 48
+PREPARE_UNROLL = 8
+FINISH_UNROLL = 4
 REST = 16
 SELF_UNROLL = 16
 EXTRA_ROWS = 8
@@ -111,7 +113,7 @@
     )(ok, spectra, model)
 
 
-def band_kernel(limits_ref, ok_ref, before_ref, x_ref, out_ref, mis_ref, wt_ref, at_ref, acc_ref, own_ref, far_ref, r0_ref, r1_ref, t0_ref, t1_ref, *, firsts, wrap, pack):
+def band_kernel(limits_ref, ok_ref, before_ref, x_ref, out_ref, mis_ref, wt_ref, at_ref, acc_ref, own_ref, far_ref, r0_ref, r1_ref, t0_ref, t1_ref, live_ref, *, firsts, wrap, pack):
     blocks, bins, rows, width = x_ref.shape
     unroll = max(2, UNROLL // bins // 2 * 2)
     rest = max(2, REST // bins // 2 * 2)
@@ -130,10 +132,10 @@
         far_ref[b] = jnp.zeros_like(far_ref[b])
         return carry
 
-    lax.fori_loop(0, blocks, prepare, 0, unroll=math.gcd(blocks, 4))
-
-    row = lax.broadcasted_iota(jnp.int32, (width, 2 * width), 0)
-    col = lax.broadcasted_iota(jnp.int32, (width, 2 * width), 1) % width
+    lax.fori_loop(0, blocks, prepare, 0, unroll=math.gcd(blocks, PREPARE_UNROLL))
+
+    row = lax.broadcasted_iota(jnp.int32, (width, width), 0)
+    col = lax.broadcasted_iota(jnp.int32, (width, width), 1)
     diff = col - row
 
     def last_piece(b):
@@ -152,12 +154,13 @@
 
     def cross(slot, item):
         b, s = item
-        live = b < firsts
+        some = b < firsts
         b, j = blocks_of(b, s)
-        mask = diff <= jnp.where(live, limits_ref[b] - s * width, -width)
+        live_ref[slot] = jnp.where(diff <= jnp.where(some, limits_ref[b] - s * width, -width), 1.0, 0.0)
         for f in range(bins):
             r = jnp.dot(at_ref[b, f], wt_ref[j, f], preferred_element_type=jnp.float32)
-            r = jnp.where(mask, r, 0.0)
+            live = live_ref[slot]
+            r = jnp.concatenate([r[:, :width] * live, r[:, width:] * live], axis=1)
             acc_ref[f] += squares(r)
             r = r.astype(jnp.bfloat16)
             slots[slot][f] = r
@@ -203,7 +206,7 @@
         out_ref[b] = scaled_rows(result, mis_ref[...]) if pack else result
         return carry
 
-    lax.fori_loop(0, blocks, finish, 0, unroll=math.gcd(blocks, 2))
+    lax.fori_loop(0, blocks, finish, 0, unroll=math.gcd(blocks, FINISH_UNROLL))
 
 
 def band_call(limits, ok, before, x, firsts, wrap, pack):
@@ -229,6 +232,7 @@
             pltpu.VMEM((bins, width, 2 * width), jnp.bfloat16),
             pltpu.VMEM((bins, width, 2 * width), jnp.bfloat16),
             pltpu.VMEM((bins, width, 2 * width), jnp.bfloat16),
+            pltpu.VMEM((2, width, width), jnp.float32),
         ],
         compiler_params=pltpu.CompilerParams(vmem_limit_bytes=40 * 2**20),
         name="band",

time: 103 us -> 104 us (level)
  Pallas kernels: 43 us -> 44.2 us
    pallas_call x2, Pallas kernels: 34.7 us -> 35.9 us  [band_call(): pl.pallas_call(functools.partial(band_kernel, firsts=firsts, wrap=wrap, p...]
  transfers between devices with their start and end apart: 5 -> 5, of which waited for: 4 -> 3; matrix products, arithmetic and copies ran while one was open for 4% -> 4% of each run, Pallas kernels for 41% -> 42%
where the time goes in v1:
time: 104 us; the launch traced here: 105 us
  Pallas kernels  44.2 us (42%)
  starting transfers between devices  27 us (26%)
  waiting for transfers between devices  24.2 us (23%)
  other arithmetic  5.16 us (5%)
  between operations  3.13 us (3%)
  local copies, waits for them, and re-layouts  1.45 us (1%)
    pallas_call x2, Pallas kernels, band_call(): pl.pallas_call(functools.partial(band_kernel, firsts=firsts, wrap=wrap, p...  35.9 us
    all_to_all x4, starting transfers between devices, swap(): return lax.all_to_all(x, 'chan', 0, 0, axis_index_groups=groups, tiled=True)  27 us
    all_to_all x4, waiting for transfers between devices, swap(): return lax.all_to_all(x, 'chan', 0, 0, axis_index_groups=groups, tiled=True)  23.4 us
    pallas_call x1, Pallas kernels, self_call(): pl.pallas_call(functools.partial(self_kernel, unroll=math.gcd(bin_total,...  8.3 us
  transfers between devices with their start and end apart: 5, of which 3 were waited for; matrix products, arithmetic and copies ran while one was open for 4% of the time, Pallas kernels for 42%

profile of v1, /device:TPU:0, one launch (start us, length us, event | category | flops | bytes accessed | tf_op | source)
XLA Modules:
  0.0 105.1 jit_solution(2730855732752876145)
XLA Ops:
  0.6 0.0 slice-start
  0.6 1.0 slice_bitcast_fusion
  1.7 0.1 slice-done
  1.8 0.0 copy-start.2
  1.8 0.0 copy-start
  1.8 0.0 copy-start.1
  1.8 1.0 pad_maximum_fusion.1
  2.7 8.3 %all-to-all-start.1 = ((bf16[64,48,128]{2,1,0:T(8,128)(2,1)}), bf16[64,48,128]{2,1,0:T(8,128)(2,1)S(1)}, u32[]{:S(2)}, u32[]{:S(2)}) async-start(bf16[64,48,128]{2,1,0:T(8,128)(2,1)} %pad_maximum_fusion.1), calls=%async_computation.1 | async-start | bytes 1572864 | tf_op jit(solution)/shard_map/all_to_all | solution.py:277
  11.1 0.0 copy-done.2
  11.1 0.0 copy-done
  11.1 0.0 copy-done.1
  11.1 8.3 %own_block.1 = (f32[128,32,128]{2,1,0:T(8,128)}, f32[8,256]{1,0:T(8,128)S(1)}) custom-call(s32[1,128]{1,0:T(1,128)S(1)} %fusion.12.ok_ref, bf16[128,32,128]{2,1,0:T(8,128)(2,1)S(1)} %bitcast.17, bf16[128,16,128]{2,1,0:T(8,128)(2,1)S(1)} %bitcast.22), custom_call_target="tpu_custom_call" | custom-call | tf_op jit(solution)/shard_map/own_block/pallas_call | solution.py:103
  19.5 0.0 copy-start.3
  19.5 0.9 pad_maximum_fusion
  20.4 10.4 %all-to-all-done.1 = bf16[64,48,128]{2,1,0:T(8,128)(2,1)S(1)} async-done(((bf16[64,48,128]{2,1,0:T(8,128)(2,1)}), bf16[64,48,128]{2,1,0:T(8,128)(2,1)S(1)}, u32[]{:S(2)}, u32[]{:S(2)}) %all-to-all-start.1) | async-done | bytes 786464 | tf_op jit(solution)/shard_map/all_to_all | solution.py:277
  30.8 4.9 %all-to-all-start = ((bf16[64,48,128]{2,1,0:T(8,128)(2,1)}), bf16[64,48,128]{2,1,0:T(8,128)(2,1)S(1)}, u32[]{:S(2)}, u32[]{:S(2)}) async-start(bf16[64,48,128]{2,1,0:T(8,128)(2,1)} %pad_maximum_fusion), calls=%async_computation | async-start | bytes 1572864 | tf_op jit(solution)/shard_map/all_to_all | solution.py:277
  35.7 0.0 copy-done.3
  35.7 17.7 %band.2 = (f32[16,136,128]{2,1,0:T(8,128)S(1)}, f32[8,256]{1,0:T(8,128)S(1)}) custom-call(s32[16]{0:T(128)S(1)} %copy-done.3, s32[16,1,128]{2,1,0:T(1,128)S(1)} %bitcast.25, f32[8,256]{1,0:T(8,128)S(1)} %get-tuple-element.13.before_ref, bf16[16,4,48,128]{3,2,1,0:T(8,128)(2,1)S(1)} %bitcast.20), custom_call_target="tpu_custom_call" | custom-call | tf_op jit(solution)/shard_map/band/pallas_call | solution.py:217
  53.4 0.9 convert_element_type.30
  54.3 0.1 all-to-all-done
  54.3 6.8 %all-to-all-start.2 = ((f16[16,136,128]{2,1,0:T(8,128)(2,1)}), f16[16,136,128]{2,1,0:T(8,128)(2,1)S(1)}, u32[]{:S(2)}, u32[]{:S(2)}) async-start(f16[16,136,128]{2,1,0:T(8,128)(2,1)} %convert_element_type.30), calls=%async_computation.2 | async-start | bytes 1114112 | tf_op jit(solution)/shard_map/all_to_all | solution.py:277
  61.2 18.2 %band.3 = (f32[16,136,128]{2,1,0:T(8,128)S(1)}, f32[8,256]{1,0:T(8,128)}) custom-call(s32[16]{0:T(128)S(1)} %copy-done.3, s32[16,1,128]{2,1,0:T(1,128)S(1)} %bitcast.26, f32[8,256]{1,0:T(8,128)S(1)} %get-tuple-element.18.before_ref, bf16[16,4,48,128]{3,2,1,0:T(8,128)(2,1)S(1)} %bitcast.21), custom_call_target="tpu_custom_call" | custom-call | tf_op jit(solution)/shard_map/band/pallas_call | solution.py:217
  79.4 0.0 copy-start.4
  79.4 0.9 convert_element_type.32
  80.3 0.0 all-to-all-done.2
  80.3 6.9 %all-to-all-start.3 = ((f16[16,136,128]{2,1,0:T(8,128)(2,1)}), f16[16,136,128]{2,1,0:T(8,128)(2,1)S(1)}, u32[]{:S(2)}, u32[]{:S(2)}) async-start(f16[16,136,128]{2,1,0:T(8,128)(2,1)} %convert_element_type.32), calls=%async_computation.3 | async-start | bytes 1114112 | tf_op jit(solution)/shard_map/all_to_all | solution.py:277
  87.2 0.1 slice.64
  87.3 0.0 copy-done.4
  87.4 0.4 fusion.2
  87.7 13.0 %all-to-all-done.3 = f16[16,136,128]{2,1,0:T(8,128)(2,1)S(1)} async-done(((f16[16,136,128]{2,1,0:T(8,128)(2,1)}), f16[16,136,128]{2,1,0:T(8,128)(2,1)S(1)}, u32[]{:S(2)}, u32[]{:S(2)}) %all-to-all-start.3) | async-done | bytes 557088 | tf_op jit(solution)/shard_map/all_to_all | solution.py:277
  100.7 0.6 fusion.11
  101.4 0.0 collective-permute-start
  101.4 0.1 slice.66
  101.6 0.4 fusion
  101.9 0.0 copy-start.5
  102.0 0.8 collective-permute-done
  104.0 0.0 copy-done.5
  (5 shorter events, 0.1 us)
Async XLA Ops:
  0.6 1.1 %slice-start = ((bf16[128,2,16,128]{3,2,1,0:T(8,128)(2,1)}), bf16[64,2,16,128]{3,2,1,0:T(8,128)(2,1)S(1)}, s32[]{:S(2)}) async-start(bf16[128,2,16,128]{3,2,1,0:T(8,128)(2,1)} %param.4), calls=%async_computation.4 | async-start | bytes 1048576 | tf_op jit(solution)/shard_map/slice | solution.py:288
  1.8 9.3 %copy-start.2 = (s32[2048]{0:T(1024)S(1)}, s32[2048]{0:T(1024)}, u32[]{:S(2)}) copy-start(s32[2048]{0:T(1024)} %param.6) | copy-start | bytes 24580
  1.8 9.3 %copy-start = (bf16[128,2,16,128]{3,2,1,0:T(8,128)(2,1)S(1)}, bf16[128,2,16,128]{3,2,1,0:T(8,128)(2,1)}, u32[]{:S(2)}) copy-start(bf16[128,2,16,128]{3,2,1,0:T(8,128)(2,1)} %param.4) | copy-start | bytes 3145732
  1.8 9.3 %copy-start.1 = (bf16[128,2,8,128]{3,2,1,0:T(8,128)(2,1)S(1)}, bf16[128,2,8,128]{3,2,1,0:T(8,128)(2,1)}, u32[]{:S(2)}) copy-start(bf16[128,2,8,128]{3,2,1,0:T(8,128)(2,1)} %param.5) | copy-start | bytes 1572868
  2.7 28.1 %all-to-all-start.1 = ((bf16[64,48,128]{2,1,0:T(8,128)(2,1)}), bf16[64,48,128]{2,1,0:T(8,128)(2,1)S(1)}, u32[]{:S(2)}, u32[]{:S(2)}) async-start(bf16[64,48,128]{2,1,0:T(8,128)(2,1)} %pad_maximum_fusion.1), calls=%async_computation.1 | async-start | bytes 1572864 | tf_op jit(solution)/shard_map/all_to_all | solution.py:277
  19.5 16.2 %copy-start.3 = (s32[16]{0:T(128)S(1)}, s32[16]{0:T(128)}, u32[]{:S(2)}) copy-start(s32[16]{0:T(128)} %limits_ref.3) | copy-start | bytes 196
  30.8 23.5 %all-to-all-start = ((bf16[64,48,128]{2,1,0:T(8,128)(2,1)}), bf16[64,48,128]{2,1,0:T(8,128)(2,1)S(1)}, u32[]{:S(2)}, u32[]{:S(2)}) async-start(bf16[64,48,128]{2,1,0:T(8,128)(2,1)} %pad_maximum_fusion), calls=%async_computation | async-start | bytes 1572864 | tf_op jit(solution)/shard_map/all_to_all | solution.py:277
  54.3 25.9 %all-to-all-start.2 = ((f16[16,136,128]{2,1,0:T(8,128)(2,1)}), f16[16,136,128]{2,1,0:T(8,128)(2,1)S(1)}, u32[]{:S(2)}, u32[]{:S(2)}) async-start(f16[16,136,128]{2,1,0:T(8,128)(2,1)} %convert_element_type.30), calls=%async_computation.2 | async-start | bytes 1114112 | tf_op jit(solution)/shard_map/all_to_all | solution.py:277
  79.4 8.0 %copy-start.4 = (f32[128,32,128]{2,1,0:T(8,128)S(1)}, f32[128,32,128]{2,1,0:T(8,128)}, u32[]{:S(2)}) copy-start(f32[128,32,128]{2,1,0:T(8,128)} %get-tuple-element.12) | copy-start | bytes 6291460
  80.3 20.5 %all-to-all-start.3 = ((f16[16,136,128]{2,1,0:T(8,128)(2,1)}), f16[16,136,128]{2,1,0:T(8,128)(2,1)S(1)}, u32[]{:S(2)}, u32[]{:S(2)}) async-start(f16[16,136,128]{2,1,0:T(8,128)(2,1)} %convert_element_type.32), calls=%async_computation.3 | async-start | bytes 1114112 | tf_op jit(solution)/shard_map/all_to_all | solution.py:277
  101.4 1.4 %collective-permute-start = (f32[]{:T(128)}, f32[]{:T(128)}, u32[]{:S(2)}, u32[]{:S(2)}) collective-permute-start(f32[]{:T(128)} %fusion.11), channel_id=1, source_target_pairs={{0,1},{1,0},{2,3},{3,2},{4,5},{5,4},{6,7},{7,6},{8,9},{9,8},{10,11... | collective-permute-start | bytes 20 | tf_op jit(solution)/shard_map/ppermute | solution.py:249
  101.9 2.0 %copy-start.5 = (f32[128,32,128]{2,1,0:T(8,128)}, f32[128,32,128]{2,1,0:T(8,128)S(1)}, u32[]{:S(2)}) copy-start(f32[128,32,128]{2,1,0:T(8,128)S(1)} %fusion) | copy-start | bytes 6291460
